TPU v7x, 32 devices: a whole 2x2x4 slice. The times are simulated.
32 devices in a mesh: bed: 8 (over y, x, core), layer: 4 (over z).
Axes of the slice: x: 2, y: 2, z: 4, core: 2. Of those that a mesh axis runs over, the one named last changes fastest.
Arguments:
- concentration: float32 [8, 1024, 4096], P('layer', 'bed'), may hold values from 0.2 to 2
- east_velocity: bfloat16 [8, 1024, 4096], P('layer', 'bed'), may hold values from -3 to 3
- north_velocity: bfloat16 [8, 1024, 4096], P('layer', 'bed'), may hold values from -3 to 3
- settling: float32 [1024, 4096], P('bed'), may hold values from 0.02 to 0.15
- surface: float32 [1024, 4096], P('bed'), may hold values from 1.8 to 6
- bed_level: float32 [1024, 4096], P('bed'), may hold values from -1 to 1
- erosion: float32 [1024, 4096], P('bed'), may hold values from 0 to 0.08
- wet_mask: int32 [1024, 4096], P('bed'), may hold values 0 or 1
Outputs:
- new_concentration: float32 [8, 1024, 4096], P('layer', 'bed')
- new_bed: float32 [1024, 4096], P('bed')
Inputs may be any that keep to these rules, and one draw needn't show every extreme that they name: `wet_mask`: 1 marks a wet cell, 0 a dry one.
All inputs are finite; a program needn't handle non-finite values. No bound on the sum of `wet_mask` on one device may be relied on, other than what follows from the above.
Results may differ from a plain program's by a relative error of at most 0.0003.
Values sent between devices are 32-bit elements; how exact they have to be, the bound alone decides.
A program may use at most 128 MiB of HBM per device.

v0:
```python
import jax
import jax.numpy as jnp
from jax import lax
from jax.sharding import PartitionSpec as P

SWEEPS = 4
ADVECT_RATE = 0.1
FLUX_GAIN = 0.15
POROSITY_GAIN = 1.0 / 0.6
RELAX_RATE = 0.2
CRIT_SLOPE = 0.5
DEPTH_FLOOR = 1.0


def padded(block, sides, width):
    for axis, dim in sides:
        count = lax.axis_size(axis)
        forward = [(i, i + 1) for i in range(count - 1)]
        backward = [(target, source) for source, target in forward]
        low = lax.ppermute(
            lax.slice_in_dim(block, block.shape[dim] - width, None, axis=dim), axis, forward
        )
        high = lax.ppermute(lax.slice_in_dim(block, 0, width, axis=dim), axis, backward)
        block = jnp.concatenate([low, block, high], axis=dim)
    return block


def passed_along(block, axis, distance):
    devices = range(lax.axis_size(axis))
    route = [(i - distance, i) for i in devices if i - distance in devices]
    return lax.ppermute(block, axis, route)


def face_divergence(values, speeds, which_axis):
    length_here = values.shape[which_axis]
    left_val = lax.slice_in_dim(values, 0, length_here - 1, axis=which_axis)
    right_val = lax.slice_in_dim(values, 1, length_here, axis=which_axis)
    left_spd = lax.slice_in_dim(speeds, 0, length_here - 1, axis=which_axis)
    right_spd = lax.slice_in_dim(speeds, 1, length_here, axis=which_axis)
    face_speed = 0.5 * (left_spd + right_spd)
    face_flux = jnp.maximum(face_speed, 0.0) * left_val + jnp.minimum(face_speed, 0.0) * right_val
    return lax.slice_in_dim(face_flux, 1, length_here - 1, axis=which_axis) - lax.slice_in_dim(
        face_flux, 0, length_here - 2, axis=which_axis
    )


def slide_sweep(height, wetness):
    drop_x = height[:-1, :] - height[1:, :]
    move_x = (
        RELAX_RATE
        * (drop_x - jnp.clip(drop_x, -CRIT_SLOPE, CRIT_SLOPE))
        * wetness[:-1, :]
        * wetness[1:, :]
    )
    drop_y = height[:, :-1] - height[:, 1:]
    move_y = (
        RELAX_RATE
        * (drop_y - jnp.clip(drop_y, -CRIT_SLOPE, CRIT_SLOPE))
        * wetness[:, :-1]
        * wetness[:, 1:]
    )
    return (
        height[1:-1, 1:-1]
        - move_x[1:, 1:-1]
        + move_x[:-1, 1:-1]
        - move_y[1:-1, 1:]
        + move_y[1:-1, :-1]
    )


def edge_pair(field):
    return jnp.concatenate([field[:, :1], field[:, -1:]], 1)


def body(
    concentration, east_velocity, north_velocity, settling, surface, bed_level, erosion, wet_mask
):
    layers_here = concentration.shape[0]
    layer_count = layers_here * lax.axis_size("layer")
    layer_index = lax.axis_index("layer")
    water_depth = surface - bed_level
    layer_thick = water_depth / layer_count
    east_speed = east_velocity.astype(jnp.float32)
    north_speed = north_velocity.astype(jnp.float32)
    flux_east = east_speed * concentration * layer_thick
    flux_north = north_speed * concentration * layer_thick
    edges = jnp.stack([edge_pair(concentration), edge_pair(east_speed), edge_pair(flux_east)])
    rims = padded(edges, (("bed", 2),), 1)
    before = rims[:, :, :1]
    after = rims[:, :, 3:]
    conc_along = jnp.concatenate([before[0], concentration, after[0]], 1)
    speed_along = jnp.concatenate([before[1], east_speed, after[1]], 1)
    east_wide = jnp.concatenate([before[2], flux_east, after[2]], 1)
    upper_row = passed_along(concentration[0], "layer", -1)
    pad_y = ((0, 0), (0, 0), (1, 1))
    advect = face_divergence(conc_along, speed_along, 1) + face_divergence(
        jnp.pad(concentration, pad_y), jnp.pad(north_speed, pad_y), 2
    )
    bottom_flag = (layer_index == 0).astype(jnp.float32)
    falling = jnp.concatenate([concentration[1:], upper_row[None]], 0) * settling
    source = falling - settling * concentration
    source = source.at[0].add(bottom_flag * erosion)
    settled = concentration - ADVECT_RATE * advect + layer_count / water_depth * source
    north_wide = jnp.pad(flux_north, pad_y)
    spread = 0.5 * (
        east_wide[:, 2:, :] - east_wide[:, :-2, :] + north_wide[:, :, 2:] - north_wide[:, :, :-2]
    )
    bed_change = FLUX_GAIN * jnp.sum(spread, 0) - bottom_flag * settling * concentration[0]
    wet_float = wet_mask.astype(jnp.float32)
    rim_width, rounds = (1, SWEEPS)
    summed_flux = lax.psum(bed_change, "layer")
    height = bed_level - POROSITY_GAIN * wet_float * (summed_flux + erosion)
    side_pad = ((0, 0), (rim_width, rim_width))
    wet_wide = jnp.pad(padded(wet_float, (("bed", 0),), rim_width), side_pad)
    for round_index in range(rounds):
        height_wide = jnp.pad(padded(height, (("bed", 0),), rim_width), side_pad)
        wetness = wet_wide
        height_wide = slide_sweep(height_wide, wetness)
        wetness = wetness[1:-1, 1:-1]
        height = height_wide
    new_depth = jnp.maximum(surface - height, DEPTH_FLOOR)
    return (settled * (water_depth / new_depth), height)


def solution(mesh):
    in_specs = (
        P("layer", "bed", None),
        P("layer", "bed", None),
        P("layer", "bed", None),
        P("bed", None),
        P("bed", None),
        P("bed", None),
        P("bed", None),
        P("bed", None),
    )
    out_specs = (P("layer", "bed", None), P("bed", None))
    return jax.shard_map(body, mesh=mesh, in_specs=in_specs, out_specs=out_specs, check_vma=False)
```

profile of v0, /device:TPU:4, one launch (start us, length us, event | category | flops | bytes accessed | tf_op | source)
XLA Modules:
  0.0 256.3 jit_solution(9465956623220491633)
XLA Ops:
  7.2 2.7 %fusion.39 = (f32[1,128,4096]{2,1,0:T(8,128)S(1)}, f32[128,4096]{1,0:T(8,128)S(1)}) fusion(f32[2,128,4096]{2,1,0:T(8,128)} %param.10), kind=kLoop, calls=%fused_computation.111 | loop fusion | bytes 8388608 | tf_op jit(solution)/shard_map/slice | solution.py:100
  9.9 1.6 collective-permute-start.2
  11.9 3.4 %broadcast_divide_fusion = (f32[128,4096]{1,0:T(8,128)}, f32[128,4096]{1,0:T(8,128)S(1)}) fusion(f32[128,4096]{1,0:T(8,128)} %param.14, f32[128,4096]{1,0:T(8,128)S(1)} %copy-done.16), kind=kLoop, calls=%fused_computation.99 | loop fusion | flops 1048576 | bytes 8388608 | tf_op jit(solution)/shard_map/div | solution.py:103
  15.3 1.3 copy-done.5
  16.8 42.6 %collective-permute-done.2 = f32[128,4096]{1,0:T(8,128)S(1)} collective-permute-done((f32[128,4096]{1,0:T(8,128)S(1)}, f32[128,4096]{1,0:T(8,128)S(1)}, u32[]{:S(2)}, u32[]{:S(2)}) %collective-permute-start.2) | collective-permute-done | bytes 2097184 | tf_op jit(solution)/shard_map/ppermute | solution.py:31
  59.5 4.4 %multiply_multiply_fusion = (f32[2,128,4096]{2,1,0:T(8,128)}, f32[2,128,4096]{2,1,0:T(8,128)S(1)}, f32[2,128,4096]{2,1,0:T(8,128)}) fusion(f32[2,128,4096]{2,1,0:T(8,128)S(1)} %copy-done, f32[128,4096]{1,0:T(8,128)S(1)} %broadcast_multiply_fusion, bf16[2,128,4096]{2,1,0:T(8,128)(2,1)S(1)} %copy-done.11, bf16[2,128,4096]{2,1,0:T(8,128)(2,1)S(1)} %copy-done.8, ...), kind=kLoop, calls=%fused_computation.22 | loop fusion | flops 10485760 | bytes 29360128 | tf_op jit(solution)/shard_map/mul | solution.py:86
  63.9 2.0 copy-done.6
  66.3 1.9 collective-permute-start.1
  68.2 2.4 collective-permute-start
  70.7 4.4 %collective-permute-done = f32[3,2,1,4096]{3,2,1,0:T(1,128)S(1)} collective-permute-done((f32[3,2,1,4096]{3,2,1,0:T(1,128)S(1)}, f32[3,2,1,4096]{3,2,1,0:T(1,128)S(1)}, u32[]{:S(2)}, u32[]{:S(2)}) %collective-permute-start) | collective-permute-done | bytes 98336 | tf_op jit(solution)/shard_map/ppermute | solution.py:20
  75.1 8.3 %fusion.6 = f32[128,4096]{1,0:T(8,128)S(1)} fusion(f32[2,128,4096]{2,1,0:T(8,128)} %copy-done.6, f32[2,1,4096]{2,1,0:T(1,128)S(1)} %get-tuple-element.44, f32[2,1,4096]{2,1,0:T(1,128)S(1)} %get-tuple-element.41, f32[2,128,4096]{2,1,0:T(8,128)} %get-tuple-element.18), kind=kLoop, calls=%fused_computation.11 | loop fusion | flops 6815744 | bytes 10551296 | tf_op jit(solution)/shard_map/reduce_sum | solution.py:108
  83.4 1.8 multiply_subtract_fusion.1
  85.3 1.9 convert_element_type.25
  87.2 1.4 copy-done.9
  88.6 1.9 collective-permute-start.5
  90.6 4.5 %collective-permute-start.6 = (f32[1,4096]{1,0:T(1,128)S(1)}, f32[1,4096]{1,0:T(1,128)S(1)}, u32[]{:S(2)}, u32[]{:S(2)}) collective-permute-start(f32[1,4096]{1,0:T(1,128)S(1)} %get-tuple-element.34), channel_id=1, source_target_pairs={{4,0},{8,4},{12,8},{16,12},{20,16},{24,20},{28,24},{5,1},{9,5},{13... | collective-permute-start | bytes 49160 | tf_op jit(solution)/shard_map/ppermute | solution.py:23
  95.1 2.5 convert_element_type.23
  97.6 73.6 %all-reduce.10.cloned.1.call-done = f32[128,4096]{1,0:T(8,128)} async-done(((f32[128,4096]{1,0:T(8,128)}), f32[128,4096]{1,0:T(8,128)}) %all-reduce.10.cloned.1.call-update) | async-done | bytes 2097168 | tf_op jit(solution)/shard_map/psum | solution.py:111
  171.2 4.2 %multiply_subtract_fusion = f32[128,4096]{1,0:T(8,128)S(1)} fusion(f32[128,4096]{1,0:T(8,128)} %param.15, f32[128,4096]{1,0:T(8,128)} %all-reduce.10.cloned.1.call-done, f32[128,4096]{1,0:T(8,128)} %param.16, s32[128,4096]{1,0:T(8,128)} %param.17), kind=kLoop, calls=%fused_computation.96 | loop fusion | flops 2621440 | bytes 10485760 | tf_op jit(solution)/shard_map/sub | solution.py:112
  175.5 1.9 collective-permute-start.3
  177.4 4.5 %collective-permute-start.4 = (f32[1,4096]{1,0:T(1,128)S(1)}, f32[1,4096]{1,0:T(1,128)S(1)}, u32[]{:S(2)}, u32[]{:S(2)}) collective-permute-start(f32[1,4096]{1,0:T(1,128)S(1)} %get-tuple-element.36), channel_id=1, source_target_pairs={{4,0},{8,4},{12,8},{16,12},{20,16},{24,20},{28,24},{5,1},{9,5},{13... | collective-permute-start | bytes 49160 | tf_op jit(solution)/shard_map/ppermute | solution.py:23
  182.0 0.7 select_maximum_fusion.6
  183.4 0.7 select_maximum_fusion.8
  184.1 0.8 fusion.15
  184.9 1.3 fusion.18
  186.2 1.8 slice_add_fusion.6
  188.0 2.7 %collective-permute-start.7 = (f32[1,4096]{1,0:T(1,128)S(1)}, f32[1,4096]{1,0:T(1,128)S(1)}, u32[]{:S(2)}, u32[]{:S(2)}) collective-permute-start(f32[1,4096]{1,0:T(1,128)S(1)} %get-tuple-element.31), channel_id=1, source_target_pairs={{0,4},{4,8},{8,12},{12,16},{16,20},{20,24},{24,28},{1,5},{5,9},{9,... | collective-permute-start | bytes 49160 | tf_op jit(solution)/shard_map/ppermute | solution.py:20
  190.8 4.1 %collective-permute-start.8 = (f32[1,4096]{1,0:T(1,128)S(1)}, f32[1,4096]{1,0:T(1,128)S(1)}, u32[]{:S(2)}, u32[]{:S(2)}) collective-permute-start(f32[1,4096]{1,0:T(1,128)S(1)} %get-tuple-element.32), channel_id=1, source_target_pairs={{4,0},{8,4},{12,8},{16,12},{20,16},{24,20},{28,24},{5,1},{9,5},{13... | collective-permute-start | bytes 49160 | tf_op jit(solution)/shard_map/ppermute | solution.py:23
  194.9 2.4 multiply_add_fusion
  197.3 2.5 convert_element_type.22
  200.5 0.8 fusion.21
  201.3 1.3 fusion.24
  202.6 1.8 slice_add_fusion.4
  204.4 2.4 collective-permute-start.10
  206.8 1.9 collective-permute-start.9
  209.4 3.4 %collective-permute-done.9 = f32[1,4096]{1,0:T(1,128)S(1)} collective-permute-done((f32[1,4096]{1,0:T(1,128)S(1)}, f32[1,4096]{1,0:T(1,128)S(1)}, u32[]{:S(2)}, u32[]{:S(2)}) %collective-permute-start.9) | collective-permute-done | bytes 16416 | tf_op jit(solution)/shard_map/ppermute | solution.py:20
  212.8 0.7 select_maximum_fusion.2
  213.5 0.8 fusion.27
  214.3 1.3 fusion.30
  215.6 1.9 slice_add_fusion.2
  217.5 1.9 collective-permute-start.11
  219.4 4.8 %collective-permute-start.12 = (f32[1,4096]{1,0:T(1,128)S(1)}, f32[1,4096]{1,0:T(1,128)S(1)}, u32[]{:S(2)}, u32[]{:S(2)}) collective-permute-start(f32[1,4096]{1,0:T(1,128)S(1)} %get-tuple-element.28), channel_id=1, source_target_pairs={{4,0},{8,4},{12,8},{16,12},{20,16},{24,20},{28,24},{5,1},{9,5},{13... | collective-permute-start | bytes 49160 | tf_op jit(solution)/shard_map/ppermute | solution.py:23
  224.2 5.1 %fusion.1 = f32[2,129,4096]{2,1,0:T(8,128)S(1)} fusion(f32[2,128,4096]{2,1,0:T(8,128)S(1)} %copy-done.2, f32[2,1,4096]{2,1,0:T(1,128)S(1)} %get-tuple-element.45, f32[2,1,4096]{2,1,0:T(1,128)S(1)} %get-tuple-element.42, f32[2,1,4096]{2,1,0:T(1,128)S(1)} %get-tuple-element.43, f32[2,128,4096]{2,1,0:T(8,128)} %convert_element_type.22, ...), kind=kLoop, calls=%fused_computation.3 | loop fusion | flops 11624448 | bytes 12746752 | tf_op jit(solution)/shard_map/add | solution.py:41
  229.3 0.7 select_maximum_fusion
  230.0 2.2 fusion.33
  232.2 2.6 %fusion.36 = f32[130,4097]{1,0:T(8,128)} fusion(f32[130,4098]{1,0:T(8,128)S(1)} %select_maximum_fusion, f32[130,4098]{1,0:T(8,128)S(1)} %select_maximum_fusion.6), kind=kLoop, calls=%fused_computation.57 | loop fusion | flops 3195660 | bytes 10652200 | tf_op jit(solution)/shard_map/mul | solution.py:57
  234.9 9.2 %maximum_divide_fusion = (f32[128,4096]{1,0:T(8,128)}, f32[128,4096]{1,0:T(8,128)}) fusion(f32[128,4096]{1,0:T(8,128)} %copy-done.5, f32[128,4096]{1,0:T(8,128)} %param.14, f32[130,4097]{1,0:T(8,128)} %fusion.36, f32[129,4098]{1,0:T(8,128)} %fusion.33, f32[128,4096]{1,0:T(8,128)} %copy-done.4), kind=kLoop, calls=%fused_computation.95 | loop fusion | flops 3670016 | bytes 18874368 | tf_op jit(solution)/shard_map/div | solution.py:122
  244.0 5.4 %fusion.11 = f32[2,128,4096]{2,1,0:T(8,128)} fusion(f32[2,128,4096]{2,1,0:T(8,128)S(1)} %copy-done.2, f32[2,128,4097]{2,1,0:T(8,128)S(1)} %multiply_add_fusion, f32[2,129,4096]{2,1,0:T(8,128)S(1)} %fusion.1, f32[2,128,4096]{2,1,0:T(8,128)S(1)} %fusion.38, f32[128,4096]{1,0:T(8,128)} %get-tuple-element.16, f32[128,4096]{1,0:T(8,128)} %get-tuple-element.14), kind=kLoop, calls=%fused_computation.18 | loop fusion | flops 8388608 | bytes 33554432 | tf_op jit(solution)/shard_map/mul | solution.py:122
  (60 shorter events, 3.2 us)
Async XLA Ops:
  7.2 4.4 %copy-start.8 = (bf16[2,128,4096]{2,1,0:T(8,128)(2,1)S(1)}, bf16[2,128,4096]{2,1,0:T(8,128)(2,1)}, u32[]{:S(2)}) copy-start(bf16[2,128,4096]{2,1,0:T(8,128)(2,1)} %param.11) | copy-start | bytes 6291460
  7.2 164.1 %all-reduce.10.cloned.1.call-start = ((), (), s32[]{:S(2)}) async-start(), calls=%async_computation | async-start | bytes 4194304 | tf_op jit(solution)/shard_map/psum | solution.py:111
  7.2 4.3 %copy-start = (f32[2,128,4096]{2,1,0:T(8,128)S(1)}, f32[2,128,4096]{2,1,0:T(8,128)}, u32[]{:S(2)}) copy-start(f32[2,128,4096]{2,1,0:T(8,128)} %param.10) | copy-start | bytes 12582916
  7.2 4.7 %copy-start.16 = (f32[128,4096]{1,0:T(8,128)S(1)}, f32[128,4096]{1,0:T(8,128)}, u32[]{:S(2)}) copy-start(f32[128,4096]{1,0:T(8,128)} %param.15) | copy-start | bytes 6291460
  9.9 49.5 %collective-permute-start.2 = (f32[128,4096]{1,0:T(8,128)S(1)}, f32[128,4096]{1,0:T(8,128)S(1)}, u32[]{:S(2)}, u32[]{:S(2)}) collective-permute-start(f32[128,4096]{1,0:T(8,128)S(1)} %get-tuple-element.22), channel_id=1, source_target_pairs={{1,0},{2,1},{3,2},{5,4},{6,5},{7,6},{9,8},{10,9},{11,10},{13,12},{... | collective-permute-start | bytes 6291464 | tf_op jit(solution)/shard_map/ppermute | solution.py:31
  15.3 1.3 copy-start.5
  15.3 44.2 %copy-start.11 = (bf16[2,128,4096]{2,1,0:T(8,128)(2,1)S(1)}, bf16[2,128,4096]{2,1,0:T(8,128)(2,1)}, u32[]{:S(2)}) copy-start(bf16[2,128,4096]{2,1,0:T(8,128)(2,1)} %param.12) | copy-start | bytes 6291460
  15.3 44.2 %copy-start.13 = (f32[128,4096]{1,0:T(8,128)S(1)}, f32[128,4096]{1,0:T(8,128)}, u32[]{:S(2)}) copy-start(f32[128,4096]{1,0:T(8,128)} %param.13) | copy-start | bytes 6291460
  63.9 2.0 copy-start.6
  66.3 4.4 %collective-permute-start.1 = (f32[3,2,1,4096]{3,2,1,0:T(1,128)S(1)}, f32[3,2,1,4096]{3,2,1,0:T(1,128)S(1)}, u32[]{:S(2)}, u32[]{:S(2)}) collective-permute-start(f32[3,2,1,4096]{3,2,1,0:T(1,128)S(1)} %get-tuple-element.39), channel_id=1, source_target_pairs={{4,0},{8,4},{12,8},{16,12},{20,16},{24,20},{28,24},{5,1},{9,5},{13... | collective-permute-start | bytes 294920 | tf_op jit(solution)/shard_map/ppermute | solution.py:23
  68.2 6.8 %collective-permute-start = (f32[3,2,1,4096]{3,2,1,0:T(1,128)S(1)}, f32[3,2,1,4096]{3,2,1,0:T(1,128)S(1)}, u32[]{:S(2)}, u32[]{:S(2)}) collective-permute-start(f32[3,2,1,4096]{3,2,1,0:T(1,128)S(1)} %get-tuple-element.40), channel_id=1, source_target_pairs={{0,4},{4,8},{8,12},{12,16},{16,20},{20,24},{24,28},{1,5},{5,9},{9,... | collective-permute-start | bytes 294920 | tf_op jit(solution)/shard_map/ppermute | solution.py:20
  75.1 8.3 %copy-start.1 = (f32[2,128,4096]{2,1,0:T(8,128)S(1)}, f32[2,128,4096]{2,1,0:T(8,128)}, u32[]{:S(2)}) copy-start(f32[2,128,4096]{2,1,0:T(8,128)} %param.10) | copy-start | bytes 12582916
  75.1 8.3 %copy-start.14 = (f32[128,4096]{1,0:T(8,128)S(1)}, f32[128,4096]{1,0:T(8,128)}, u32[]{:S(2)}) copy-start(f32[128,4096]{1,0:T(8,128)} %param.13) | copy-start | bytes 6291460
  85.3 9.8 %copy-start.12 = (bf16[2,128,4096]{2,1,0:T(8,128)(2,1)S(1)}, bf16[2,128,4096]{2,1,0:T(8,128)(2,1)}, u32[]{:S(2)}) copy-start(bf16[2,128,4096]{2,1,0:T(8,128)(2,1)} %param.12) | copy-start | bytes 6291460
  87.2 1.4 copy-start.9
  88.6 93.3 %collective-permute-start.5 = (f32[1,4096]{1,0:T(1,128)S(1)}, f32[1,4096]{1,0:T(1,128)S(1)}, u32[]{:S(2)}, u32[]{:S(2)}) collective-permute-start(f32[1,4096]{1,0:T(1,128)S(1)} %get-tuple-element.33), channel_id=1, source_target_pairs={{0,4},{4,8},{8,12},{12,16},{16,20},{20,24},{24,28},{1,5},{5,9},{9,... | collective-permute-start | bytes 49160 | tf_op jit(solution)/shard_map/ppermute | solution.py:20
  90.6 91.4 %collective-permute-start.6 = (f32[1,4096]{1,0:T(1,128)S(1)}, f32[1,4096]{1,0:T(1,128)S(1)}, u32[]{:S(2)}, u32[]{:S(2)}) collective-permute-start(f32[1,4096]{1,0:T(1,128)S(1)} %get-tuple-element.34), channel_id=1, source_target_pairs={{4,0},{8,4},{12,8},{16,12},{20,16},{24,20},{28,24},{5,1},{9,5},{13... | collective-permute-start | bytes 49160 | tf_op jit(solution)/shard_map/ppermute | solution.py:23
  171.2 10.7 %copy-start.10 = (f32[128,4096]{1,0:T(8,128)S(1)}, f32[128,4096]{1,0:T(8,128)}, u32[]{:S(2)}) copy-start(f32[128,4096]{1,0:T(8,128)} %copy-done.9) | copy-start | bytes 6291460
  175.5 7.2 %collective-permute-start.3 = (f32[1,4096]{1,0:T(1,128)S(1)}, f32[1,4096]{1,0:T(1,128)S(1)}, u32[]{:S(2)}, u32[]{:S(2)}) collective-permute-start(f32[1,4096]{1,0:T(1,128)S(1)} %get-tuple-element.35), channel_id=1, source_target_pairs={{0,4},{4,8},{8,12},{12,16},{16,20},{20,24},{24,28},{1,5},{5,9},{9,... | collective-permute-start | bytes 49160 | tf_op jit(solution)/shard_map/ppermute | solution.py:20
  177.4 6.0 %collective-permute-start.4 = (f32[1,4096]{1,0:T(1,128)S(1)}, f32[1,4096]{1,0:T(1,128)S(1)}, u32[]{:S(2)}, u32[]{:S(2)}) collective-permute-start(f32[1,4096]{1,0:T(1,128)S(1)} %get-tuple-element.36), channel_id=1, source_target_pairs={{4,0},{8,4},{12,8},{16,12},{20,16},{24,20},{28,24},{5,1},{9,5},{13... | collective-permute-start | bytes 49160 | tf_op jit(solution)/shard_map/ppermute | solution.py:23
  186.2 8.7 %copy-start.2 = (f32[2,128,4096]{2,1,0:T(8,128)S(1)}, f32[2,128,4096]{2,1,0:T(8,128)}, u32[]{:S(2)}) copy-start(f32[2,128,4096]{2,1,0:T(8,128)} %param.10) | copy-start | bytes 12582916
  186.2 8.7 %copy-start.7 = (f32[2,128,4096]{2,1,0:T(8,128)S(1)}, f32[2,128,4096]{2,1,0:T(8,128)}, u32[]{:S(2)}) copy-start(f32[2,128,4096]{2,1,0:T(8,128)} %convert_element_type.23) | copy-start | bytes 12582916
  188.0 11.7 %collective-permute-start.7 = (f32[1,4096]{1,0:T(1,128)S(1)}, f32[1,4096]{1,0:T(1,128)S(1)}, u32[]{:S(2)}, u32[]{:S(2)}) collective-permute-start(f32[1,4096]{1,0:T(1,128)S(1)} %get-tuple-element.31), channel_id=1, source_target_pairs={{0,4},{4,8},{8,12},{12,16},{16,20},{20,24},{24,28},{1,5},{5,9},{9,... | collective-permute-start | bytes 49160 | tf_op jit(solution)/shard_map/ppermute | solution.py:20
  190.8 9.0 %collective-permute-start.8 = (f32[1,4096]{1,0:T(1,128)S(1)}, f32[1,4096]{1,0:T(1,128)S(1)}, u32[]{:S(2)}, u32[]{:S(2)}) collective-permute-start(f32[1,4096]{1,0:T(1,128)S(1)} %get-tuple-element.32), channel_id=1, source_target_pairs={{4,0},{8,4},{12,8},{16,12},{20,16},{24,20},{28,24},{5,1},{9,5},{13... | collective-permute-start | bytes 49160 | tf_op jit(solution)/shard_map/ppermute | solution.py:23
  202.6 6.2 %copy-start.3 = (f32[2,128,4096]{2,1,0:T(8,128)S(1)}, f32[2,128,4096]{2,1,0:T(8,128)}, u32[]{:S(2)}) copy-start(f32[2,128,4096]{2,1,0:T(8,128)} %get-tuple-element.20) | copy-start | bytes 12582916
  202.6 6.2 %copy-start.15 = (f32[128,4096]{1,0:T(8,128)S(1)}, f32[128,4096]{1,0:T(8,128)}, u32[]{:S(2)}) copy-start(f32[128,4096]{1,0:T(8,128)} %param.16) | copy-start | bytes 6291460
  204.4 5.0 %collective-permute-start.10 = (f32[1,4096]{1,0:T(1,128)S(1)}, f32[1,4096]{1,0:T(1,128)S(1)}, u32[]{:S(2)}, u32[]{:S(2)}) collective-permute-start(f32[1,4096]{1,0:T(1,128)S(1)} %get-tuple-element.30), channel_id=1, source_target_pairs={{4,0},{8,4},{12,8},{16,12},{20,16},{24,20},{28,24},{5,1},{9,5},{13... | collective-permute-start | bytes 49160 | tf_op jit(solution)/shard_map/ppermute | solution.py:23
  206.8 6.0 %collective-permute-start.9 = (f32[1,4096]{1,0:T(1,128)S(1)}, f32[1,4096]{1,0:T(1,128)S(1)}, u32[]{:S(2)}, u32[]{:S(2)}) collective-permute-start(f32[1,4096]{1,0:T(1,128)S(1)} %get-tuple-element.29), channel_id=1, source_target_pairs={{0,4},{4,8},{8,12},{12,16},{16,20},{20,24},{24,28},{1,5},{5,9},{9,... | collective-permute-start | bytes 49160 | tf_op jit(solution)/shard_map/ppermute | solution.py:20
  217.4 11.9 %copy-start.4 = (f32[128,4096]{1,0:T(8,128)}, f32[128,4096]{1,0:T(8,128)S(1)}, u32[]{:S(2)}) copy-start(f32[128,4096]{1,0:T(8,128)S(1)} %slice_add_fusion.2) | copy-start | bytes 6291460
  217.5 11.8 %collective-permute-start.11 = (f32[1,4096]{1,0:T(1,128)S(1)}, f32[1,4096]{1,0:T(1,128)S(1)}, u32[]{:S(2)}, u32[]{:S(2)}) collective-permute-start(f32[1,4096]{1,0:T(1,128)S(1)} %get-tuple-element.27), channel_id=1, source_target_pairs={{0,4},{4,8},{8,12},{12,16},{16,20},{20,24},{24,28},{1,5},{5,9},{9,... | collective-permute-start | bytes 49160 | tf_op jit(solution)/shard_map/ppermute | solution.py:20
  219.4 9.9 %collective-permute-start.12 = (f32[1,4096]{1,0:T(1,128)S(1)}, f32[1,4096]{1,0:T(1,128)S(1)}, u32[]{:S(2)}, u32[]{:S(2)}) collective-permute-start(f32[1,4096]{1,0:T(1,128)S(1)} %get-tuple-element.28), channel_id=1, source_target_pairs={{4,0},{8,4},{12,8},{16,12},{20,16},{24,20},{28,24},{5,1},{9,5},{13... | collective-permute-start | bytes 49160 | tf_op jit(solution)/shard_map/ppermute | solution.py:23
Sparse Core Ops, SparseCore 0:
  85.4 85.7 all-reduce.9
where the time goes:
time: 257 us; the launch traced here: 256 us
  waiting for transfers between devices  125 us (49%)
  other arithmetic  72.3 us (28%)
  starting transfers between devices  36.6 us (14%)
  between operations  14.6 us (6%)
  local copies, waits for them, and re-layouts  8.08 us (3%)
    psum x1, waiting for transfers between devices, body(): summed_flux = lax.psum(bed_change, 'layer')  73.6 us
    ppermute x1, waiting for transfers between devices, passed_along(): return lax.ppermute(block, axis, route)  42.6 us
    ppermute x6, starting transfers between devices, padded(): lax.ppermute(lax.slice_in_dim(block, 0, width, axis=dim), axis, backward)  22.2 us
    ppermute x6, starting transfers between devices, padded(): lax.ppermute(lax.slice_in_dim(block, block.shape[dim] - width, None, axis...  12.8 us
    div x1, other arithmetic, body(): return (settled * (water_depth / new_depth), height)  9.16 us
    reduce_sum x1, other arithmetic, body(): jnp.sum(spread, 0)  8.31 us
    ppermute x6, waiting for transfers between devices, padded(): lax.ppermute(lax.slice_in_dim(block, block.shape[dim] - width, None, axis...  7.76 us
    add x2, other arithmetic, face_divergence(): jnp.maximum(face_speed, 0.0) * left_val  7.51 us
  transfers between devices with their start and end apart: 14, of which 5 were waited for; matrix products, arithmetic and copies ran while one was open for 9% of the time, Pallas kernels for 0%

commit v1 on v0

--- a/solution.py
+++ b/solution.py
@@ -108,7 +108,13 @@
     bed_change = FLUX_GAIN * jnp.sum(spread, 0) - bottom_flag * settling * concentration[0]
     wet_float = wet_mask.astype(jnp.float32)
     rim_width, rounds = (1, SWEEPS)
-    summed_flux = lax.psum(bed_change, "layer")
+    n_dev = lax.axis_size("layer")
+    summed_flux, far = (bed_change, 1)
+    while far < n_dev:
+        summed_flux = summed_flux + lax.ppermute(
+            summed_flux, "layer", [(i_2, i_2 ^ far) for i_2 in range(n_dev)]
+        )
+        far = 2 * far
     height = bed_level - POROSITY_GAIN * wet_float * (summed_flux + erosion)
     side_pad = ((0, 0), (rim_width, rim_width))
     wet_wide = jnp.pad(padded(wet_float, (("bed", 0),), rim_width), side_pad)

time: 257 us -> 289 us (1.12)
  waiting for transfers between devices: 125 us -> 173 us
  between operations: 14.6 us -> 1.21 us
  other arithmetic: 72.3 us -> 65.4 us
  starting transfers between devices: 36.6 us -> 43.1 us
    ppermute x0 -> x2, waiting for transfers between devices: none -> 125 us  [body(): lax.ppermute(summed_flux, 'layer', [(i_2, i_2 ^ far) for i_2 in range(n_d...]
    psum x1 -> x0, waiting for transfers between devices: 73.6 us -> none  [body(): summed_flux = lax.psum(bed_change, 'layer')]
    ppermute x0 -> x2, starting transfers between devices: none -> 4.3 us  [body(): lax.ppermute(summed_flux, 'layer', [(i_2, i_2 ^ far) for i_2 in range(n_d...]
    ppermute x6, starting transfers between devices: 22.2 us -> 25.3 us  [padded(): lax.ppermute(lax.slice_in_dim(block, 0, width, axis=dim), axis, backward)]
  transfers between devices with their start and end apart: 14 -> 15, of which waited for: 5 -> 6; matrix products, arithmetic and copies ran while one was open for 9% -> 6% of each run, Pallas kernels for 0% -> 0%
where the time goes in v1:
time: 289 us; the launch traced here: 288 us
  waiting for transfers between devices  173 us (60%)
  other arithmetic  65.4 us (23%)
  starting transfers between devices  43.1 us (15%)
  local copies, waits for them, and re-layouts  5.43 us (2%)
    ppermute x2, waiting for transfers between devices, body(): lax.ppermute(summed_flux, 'layer', [(i_2, i_2 ^ far) for i_2 in range(n_d...  125 us
    ppermute x1, waiting for transfers between devices, passed_along(): return lax.ppermute(block, axis, route)  41.5 us
    ppermute x6, starting transfers between devices, padded(): lax.ppermute(lax.slice_in_dim(block, 0, width, axis=dim), axis, backward)  25.3 us
    ppermute x6, starting transfers between devices, padded(): lax.ppermute(lax.slice_in_dim(block, block.shape[dim] - width, None, axis...  12 us
    div x1, other arithmetic, body(): return (settled * (water_depth / new_depth), height)  9.17 us
    reduce_sum x1, other arithmetic, body(): jnp.sum(spread, 0)  8.5 us
    mul x4, other arithmetic, slide_sweep(): RELAX_RATE * (drop_y - jnp.clip(drop_y, -CRIT_SLOPE, CRIT_SLOPE))  6.43 us
  transfers between devices with their start and end apart: 15, of which 6 were waited for; matrix products, arithmetic and copies ran while one was open for 6% of the time, Pallas kernels for 0%

profile of v1, /device:TPU:4, one launch (start us, length us, event | category | flops | bytes accessed | tf_op | source)
XLA Modules:
  0.0 287.7 jit_solution(9026833961868159535)
XLA Ops:
  0.7 2.7 fusion.39
  3.3 1.6 collective-permute-start.2
  5.4 4.0 %broadcast_divide_fusion = (f32[128,4096]{1,0:T(8,128)}, f32[128,4096]{1,0:T(8,128)}) fusion(f32[128,4096]{1,0:T(8,128)S(1)} %copy-done.11, f32[128,4096]{1,0:T(8,128)} %param.15), kind=kLoop, calls=%fused_computation.99 | loop fusion | flops 1048576 | bytes 8388608 | tf_op jit(solution)/shard_map/div | solution.py:103
  9.4 1.9 broadcast_multiply_fusion
  11.3 41.5 %collective-permute-done.2 = f32[128,4096]{1,0:T(8,128)S(1)} collective-permute-done((f32[128,4096]{1,0:T(8,128)S(1)}, f32[128,4096]{1,0:T(8,128)S(1)}, u32[]{:S(2)}, u32[]{:S(2)}) %collective-permute-start.2) | collective-permute-done | bytes 2097184 | tf_op jit(solution)/shard_map/ppermute | solution.py:31
  52.9 4.4 %multiply_multiply_fusion = (f32[2,128,4096]{2,1,0:T(8,128)}, f32[2,128,4096]{2,1,0:T(8,128)S(1)}, f32[2,128,4096]{2,1,0:T(8,128)}) fusion(f32[2,128,4096]{2,1,0:T(8,128)S(1)} %copy-done, f32[128,4096]{1,0:T(8,128)S(1)} %broadcast_multiply_fusion, bf16[2,128,4096]{2,1,0:T(8,128)(2,1)S(1)} %copy-done.6, bf16[2,128,4096]{2,1,0:T(8,128)(2,1)S(1)} %copy-done.5, ...), kind=kLoop, calls=%fused_computation.22 | loop fusion | flops 10485760 | bytes 29360128 | tf_op jit(solution)/shard_map/mul | solution.py:86
  57.3 2.0 copy-done.4
  59.7 1.9 collective-permute-start.1
  61.6 2.4 collective-permute-start
  64.1 4.4 %collective-permute-done = f32[3,2,1,4096]{3,2,1,0:T(1,128)S(1)} collective-permute-done((f32[3,2,1,4096]{3,2,1,0:T(1,128)S(1)}, f32[3,2,1,4096]{3,2,1,0:T(1,128)S(1)}, u32[]{:S(2)}, u32[]{:S(2)}) %collective-permute-start) | collective-permute-done | bytes 98336 | tf_op jit(solution)/shard_map/ppermute | solution.py:20
  68.5 8.5 %fusion.6 = f32[128,4096]{1,0:T(8,128)S(1)} fusion(f32[2,128,4096]{2,1,0:T(8,128)} %copy-done.4, f32[2,1,4096]{2,1,0:T(1,128)S(1)} %get-tuple-element.44, f32[2,1,4096]{2,1,0:T(1,128)S(1)} %get-tuple-element.41, f32[2,128,4096]{2,1,0:T(8,128)} %get-tuple-element.18), kind=kLoop, calls=%fused_computation.11 | loop fusion | flops 6815744 | bytes 10551296 | tf_op jit(solution)/shard_map/reduce_sum | solution.py:108
  77.5 1.6 collective-permute-start.3
  79.2 44.3 %collective-permute-done.3 = f32[128,4096]{1,0:T(8,128)S(1)} collective-permute-done((f32[128,4096]{1,0:T(8,128)S(1)}, f32[128,4096]{1,0:T(8,128)S(1)}, u32[]{:S(2)}, u32[]{:S(2)}) %collective-permute-start.3) | collective-permute-done | bytes 2097184 | tf_op jit(solution)/shard_map/ppermute | solution.py:114
  123.7 2.7 collective-permute-start.4
  126.6 1.9 collective-permute-start.7
  128.5 4.8 %collective-permute-start.8 = (f32[1,4096]{1,0:T(1,128)S(1)}, f32[1,4096]{1,0:T(1,128)S(1)}, u32[]{:S(2)}, u32[]{:S(2)}) collective-permute-start(f32[1,4096]{1,0:T(1,128)S(1)} %get-tuple-element.34), channel_id=1, source_target_pairs={{4,0},{8,4},{12,8},{16,12},{20,16},{24,20},{28,24},{5,1},{9,5},{13... | collective-permute-start | bytes 49160 | tf_op jit(solution)/shard_map/ppermute | solution.py:23
  133.8 80.8 %collective-permute-done.4 = f32[128,4096]{1,0:T(8,128)} collective-permute-done((f32[128,4096]{1,0:T(8,128)S(1)}, f32[128,4096]{1,0:T(8,128)}, u32[]{:S(2)}, u32[]{:S(2)}) %collective-permute-start.4) | collective-permute-done | bytes 2097184 | tf_op jit(solution)/shard_map/ppermute | solution.py:114
  214.6 2.5 multiply_subtract_fusion
  217.2 1.9 collective-permute-start.5
  219.1 4.7 %collective-permute-start.6 = (f32[1,4096]{1,0:T(1,128)S(1)}, f32[1,4096]{1,0:T(1,128)S(1)}, u32[]{:S(2)}, u32[]{:S(2)}) collective-permute-start(f32[1,4096]{1,0:T(1,128)S(1)} %get-tuple-element.36), channel_id=1, source_target_pairs={{4,0},{8,4},{12,8},{16,12},{20,16},{24,20},{28,24},{5,1},{9,5},{13... | collective-permute-start | bytes 49160 | tf_op jit(solution)/shard_map/ppermute | solution.py:23
  223.8 0.7 select_maximum_fusion.6
  225.1 0.7 select_maximum_fusion.8
  225.8 0.8 fusion.15
  226.6 1.3 fusion.18
  227.8 1.9 slice_add_fusion.6
  229.8 4.5 %collective-permute-start.10 = (f32[1,4096]{1,0:T(1,128)S(1)}, f32[1,4096]{1,0:T(1,128)S(1)}, u32[]{:S(2)}, u32[]{:S(2)}) collective-permute-start(f32[1,4096]{1,0:T(1,128)S(1)} %get-tuple-element.32), channel_id=1, source_target_pairs={{4,0},{8,4},{12,8},{16,12},{20,16},{24,20},{28,24},{5,1},{9,5},{13... | collective-permute-start | bytes 49160 | tf_op jit(solution)/shard_map/ppermute | solution.py:23
  234.3 1.9 collective-permute-start.9
  236.3 2.4 multiply_add_fusion
  239.2 1.1 collective-permute-done.9
  240.3 0.7 select_maximum_fusion.4
  241.0 0.8 fusion.21
  241.8 1.3 fusion.24
  243.1 1.9 slice_add_fusion.4
  245.0 1.9 collective-permute-start.11
  247.0 4.8 %collective-permute-start.12 = (f32[1,4096]{1,0:T(1,128)S(1)}, f32[1,4096]{1,0:T(1,128)S(1)}, u32[]{:S(2)}, u32[]{:S(2)}) collective-permute-start(f32[1,4096]{1,0:T(1,128)S(1)} %get-tuple-element.30), channel_id=1, source_target_pairs={{4,0},{8,4},{12,8},{16,12},{20,16},{24,20},{28,24},{5,1},{9,5},{13... | collective-permute-start | bytes 49160 | tf_op jit(solution)/shard_map/ppermute | solution.py:23
  251.7 2.3 fusion.38
  254.1 0.7 select_maximum_fusion.2
  254.8 0.8 fusion.27
  255.6 1.3 fusion.30
  256.8 1.9 slice_add_fusion.2
  258.7 1.9 collective-permute-start.13
  260.7 4.5 %collective-permute-start.14 = (f32[1,4096]{1,0:T(1,128)S(1)}, f32[1,4096]{1,0:T(1,128)S(1)}, u32[]{:S(2)}, u32[]{:S(2)}) collective-permute-start(f32[1,4096]{1,0:T(1,128)S(1)} %get-tuple-element.28), channel_id=1, source_target_pairs={{4,0},{8,4},{12,8},{16,12},{20,16},{24,20},{28,24},{5,1},{9,5},{13... | collective-permute-start | bytes 49160 | tf_op jit(solution)/shard_map/ppermute | solution.py:23
  265.2 2.3 fusion.1
  267.6 0.7 select_maximum_fusion
  268.3 2.2 fusion.33
  270.5 2.6 fusion.36
  273.1 9.2 %maximum_divide_fusion = (f32[128,4096]{1,0:T(8,128)}, f32[128,4096]{1,0:T(8,128)}) fusion(f32[128,4096]{1,0:T(8,128)} %get-tuple-element.15, f32[128,4096]{1,0:T(8,128)} %param.14, f32[130,4097]{1,0:T(8,128)} %fusion.36, f32[129,4098]{1,0:T(8,128)} %fusion.33, f32[128,4096]{1,0:T(8,128)} %copy-done.3), kind=kLoop, calls=%fused_computation.95 | loop fusion | flops 3670016 | bytes 18874368 | tf_op jit(solution)/shard_map/div | solution.py:128
  282.3 5.4 %fusion.11 = f32[2,128,4096]{2,1,0:T(8,128)} fusion(f32[2,128,4096]{2,1,0:T(8,128)S(1)} %copy-done.1, f32[2,128,4097]{2,1,0:T(8,128)S(1)} %multiply_add_fusion, f32[2,129,4096]{2,1,0:T(8,128)S(1)} %fusion.1, f32[2,128,4096]{2,1,0:T(8,128)S(1)} %fusion.38, f32[128,4096]{1,0:T(8,128)} %get-tuple-element.16, f32[128,4096]{1,0:T(8,128)} %get-tuple-element.14), kind=kLoop, calls=%fused_computation.18 | loop fusion | flops 8388608 | bytes 33554432 | tf_op jit(solution)/shard_map/mul | solution.py:128
  (56 shorter events, 3.4 us)
Async XLA Ops:
  0.6 4.3 %copy-start = (f32[2,128,4096]{2,1,0:T(8,128)S(1)}, f32[2,128,4096]{2,1,0:T(8,128)}, u32[]{:S(2)}) copy-start(f32[2,128,4096]{2,1,0:T(8,128)} %param.10) | copy-start | bytes 12582916
  0.6 4.3 %copy-start.5 = (bf16[2,128,4096]{2,1,0:T(8,128)(2,1)S(1)}, bf16[2,128,4096]{2,1,0:T(8,128)(2,1)}, u32[]{:S(2)}) copy-start(bf16[2,128,4096]{2,1,0:T(8,128)(2,1)} %param.11) | copy-start | bytes 6291460
  0.7 4.7 %copy-start.11 = (f32[128,4096]{1,0:T(8,128)S(1)}, f32[128,4096]{1,0:T(8,128)}, u32[]{:S(2)}) copy-start(f32[128,4096]{1,0:T(8,128)} %param.14) | copy-start | bytes 6291460
  3.3 49.5 %collective-permute-start.2 = (f32[128,4096]{1,0:T(8,128)S(1)}, f32[128,4096]{1,0:T(8,128)S(1)}, u32[]{:S(2)}, u32[]{:S(2)}) collective-permute-start(f32[128,4096]{1,0:T(8,128)S(1)} %get-tuple-element.22), channel_id=1, source_target_pairs={{1,0},{2,1},{3,2},{5,4},{6,5},{7,6},{9,8},{10,9},{11,10},{13,12},{... | collective-permute-start | bytes 6291464 | tf_op jit(solution)/shard_map/ppermute | solution.py:31
  9.4 43.5 %copy-start.6 = (bf16[2,128,4096]{2,1,0:T(8,128)(2,1)S(1)}, bf16[2,128,4096]{2,1,0:T(8,128)(2,1)}, u32[]{:S(2)}) copy-start(bf16[2,128,4096]{2,1,0:T(8,128)(2,1)} %param.12) | copy-start | bytes 6291460
  9.4 43.5 %copy-start.8 = (f32[128,4096]{1,0:T(8,128)S(1)}, f32[128,4096]{1,0:T(8,128)}, u32[]{:S(2)}) copy-start(f32[128,4096]{1,0:T(8,128)} %param.13) | copy-start | bytes 6291460
  57.3 2.0 copy-start.4
  59.7 4.4 %collective-permute-start.1 = (f32[3,2,1,4096]{3,2,1,0:T(1,128)S(1)}, f32[3,2,1,4096]{3,2,1,0:T(1,128)S(1)}, u32[]{:S(2)}, u32[]{:S(2)}) collective-permute-start(f32[3,2,1,4096]{3,2,1,0:T(1,128)S(1)} %get-tuple-element.39), channel_id=1, source_target_pairs={{4,0},{8,4},{12,8},{16,12},{20,16},{24,20},{28,24},{5,1},{9,5},{13... | collective-permute-start | bytes 294920 | tf_op jit(solution)/shard_map/ppermute | solution.py:23
  61.6 6.8 %collective-permute-start = (f32[3,2,1,4096]{3,2,1,0:T(1,128)S(1)}, f32[3,2,1,4096]{3,2,1,0:T(1,128)S(1)}, u32[]{:S(2)}, u32[]{:S(2)}) collective-permute-start(f32[3,2,1,4096]{3,2,1,0:T(1,128)S(1)} %get-tuple-element.40), channel_id=1, source_target_pairs={{0,4},{4,8},{8,12},{12,16},{16,20},{20,24},{24,28},{1,5},{5,9},{9,... | collective-permute-start | bytes 294920 | tf_op jit(solution)/shard_map/ppermute | solution.py:20
  68.5 8.5 %copy-start.1 = (f32[2,128,4096]{2,1,0:T(8,128)S(1)}, f32[2,128,4096]{2,1,0:T(8,128)}, u32[]{:S(2)}) copy-start(f32[2,128,4096]{2,1,0:T(8,128)} %param.10) | copy-start | bytes 12582916
  68.5 8.5 %copy-start.9 = (f32[128,4096]{1,0:T(8,128)S(1)}, f32[128,4096]{1,0:T(8,128)}, u32[]{:S(2)}) copy-start(f32[128,4096]{1,0:T(8,128)} %param.13) | copy-start | bytes 6291460
  77.5 48.8 %copy-start.12 = (s32[128,4096]{1,0:T(8,128)S(1)}, s32[128,4096]{1,0:T(8,128)}, u32[]{:S(2)}) copy-start(s32[128,4096]{1,0:T(8,128)} %param.17) | copy-start | bytes 6291460
  77.5 45.9 %collective-permute-start.3 = (f32[128,4096]{1,0:T(8,128)S(1)}, f32[128,4096]{1,0:T(8,128)S(1)}, u32[]{:S(2)}, u32[]{:S(2)}) collective-permute-start(f32[128,4096]{1,0:T(8,128)S(1)} %multiply_subtract_fusion.1), channel_id=1, source_target_pairs={{0,1},{1,0},{2,3},{3,2},{4,5},{5,4},{6,7},{7,6},{8,9},{9,8},{10,11... | collective-permute-start | bytes 6291464 | tf_op jit(solution)/shard_map/ppermute | solution.py:114
  123.7 9.6 %copy-start.7 = (bf16[2,128,4096]{2,1,0:T(8,128)(2,1)S(1)}, bf16[2,128,4096]{2,1,0:T(8,128)(2,1)}, u32[]{:S(2)}) copy-start(bf16[2,128,4096]{2,1,0:T(8,128)(2,1)} %param.12) | copy-start | bytes 6291460
  123.7 90.9 %collective-permute-start.4 = (f32[128,4096]{1,0:T(8,128)S(1)}, f32[128,4096]{1,0:T(8,128)}, u32[]{:S(2)}, u32[]{:S(2)}) collective-permute-start(f32[128,4096]{1,0:T(8,128)S(1)} %add.85), channel_id=1, source_target_pairs={{0,2},{1,3},{2,0},{3,1},{4,6},{5,7},{6,4},{7,5},{8,10},{9,11},{10,... | collective-permute-start | bytes 6291464 | tf_op jit(solution)/shard_map/ppermute | solution.py:114
  126.6 97.3 %collective-permute-start.7 = (f32[1,4096]{1,0:T(1,128)S(1)}, f32[1,4096]{1,0:T(1,128)S(1)}, u32[]{:S(2)}, u32[]{:S(2)}) collective-permute-start(f32[1,4096]{1,0:T(1,128)S(1)} %get-tuple-element.33), channel_id=1, source_target_pairs={{0,4},{4,8},{8,12},{12,16},{16,20},{20,24},{24,28},{1,5},{5,9},{9,... | collective-permute-start | bytes 49160 | tf_op jit(solution)/shard_map/ppermute | solution.py:20
  128.5 86.1 %copy-start.10 = (f32[128,4096]{1,0:T(8,128)S(1)}, f32[128,4096]{1,0:T(8,128)}, u32[]{:S(2)}) copy-start(f32[128,4096]{1,0:T(8,128)} %param.16) | copy-start | bytes 6291460
  128.5 86.1 %copy-start.13 = (f32[128,4096]{1,0:T(8,128)S(1)}, f32[128,4096]{1,0:T(8,128)}, u32[]{:S(2)}) copy-start(f32[128,4096]{1,0:T(8,128)} %param.15) | copy-start | bytes 6291460
  128.5 95.3 %collective-permute-start.8 = (f32[1,4096]{1,0:T(1,128)S(1)}, f32[1,4096]{1,0:T(1,128)S(1)}, u32[]{:S(2)}, u32[]{:S(2)}) collective-permute-start(f32[1,4096]{1,0:T(1,128)S(1)} %get-tuple-element.34), channel_id=1, source_target_pairs={{4,0},{8,4},{12,8},{16,12},{20,16},{24,20},{28,24},{5,1},{9,5},{13... | collective-permute-start | bytes 49160 | tf_op jit(solution)/shard_map/ppermute | solution.py:23
  217.2 7.4 %collective-permute-start.5 = (f32[1,4096]{1,0:T(1,128)S(1)}, f32[1,4096]{1,0:T(1,128)S(1)}, u32[]{:S(2)}, u32[]{:S(2)}) collective-permute-start(f32[1,4096]{1,0:T(1,128)S(1)} %get-tuple-element.35), channel_id=1, source_target_pairs={{0,4},{4,8},{8,12},{12,16},{16,20},{20,24},{24,28},{1,5},{5,9},{9,... | collective-permute-start | bytes 49160 | tf_op jit(solution)/shard_map/ppermute | solution.py:20
  219.1 6.0 %collective-permute-start.6 = (f32[1,4096]{1,0:T(1,128)S(1)}, f32[1,4096]{1,0:T(1,128)S(1)}, u32[]{:S(2)}, u32[]{:S(2)}) collective-permute-start(f32[1,4096]{1,0:T(1,128)S(1)} %get-tuple-element.36), channel_id=1, source_target_pairs={{4,0},{8,4},{12,8},{16,12},{20,16},{24,20},{28,24},{5,1},{9,5},{13... | collective-permute-start | bytes 49160 | tf_op jit(solution)/shard_map/ppermute | solution.py:23
  229.8 9.4 %collective-permute-start.10 = (f32[1,4096]{1,0:T(1,128)S(1)}, f32[1,4096]{1,0:T(1,128)S(1)}, u32[]{:S(2)}, u32[]{:S(2)}) collective-permute-start(f32[1,4096]{1,0:T(1,128)S(1)} %get-tuple-element.32), channel_id=1, source_target_pairs={{4,0},{8,4},{12,8},{16,12},{20,16},{24,20},{28,24},{5,1},{9,5},{13... | collective-permute-start | bytes 49160 | tf_op jit(solution)/shard_map/ppermute | solution.py:23
  234.3 6.0 %collective-permute-start.9 = (f32[1,4096]{1,0:T(1,128)S(1)}, f32[1,4096]{1,0:T(1,128)S(1)}, u32[]{:S(2)}, u32[]{:S(2)}) collective-permute-start(f32[1,4096]{1,0:T(1,128)S(1)} %get-tuple-element.31), channel_id=1, source_target_pairs={{0,4},{4,8},{8,12},{12,16},{16,20},{20,24},{24,28},{1,5},{5,9},{9,... | collective-permute-start | bytes 49160 | tf_op jit(solution)/shard_map/ppermute | solution.py:20
  243.1 8.7 %copy-start.2 = (f32[2,128,4096]{2,1,0:T(8,128)S(1)}, f32[2,128,4096]{2,1,0:T(8,128)}, u32[]{:S(2)}) copy-start(f32[2,128,4096]{2,1,0:T(8,128)} %get-tuple-element.20) | copy-start | bytes 12582916
  245.0 9.0 %collective-permute-start.11 = (f32[1,4096]{1,0:T(1,128)S(1)}, f32[1,4096]{1,0:T(1,128)S(1)}, u32[]{:S(2)}, u32[]{:S(2)}) collective-permute-start(f32[1,4096]{1,0:T(1,128)S(1)} %get-tuple-element.29), channel_id=1, source_target_pairs={{0,4},{4,8},{8,12},{12,16},{16,20},{20,24},{24,28},{1,5},{5,9},{9,... | collective-permute-start | bytes 49160 | tf_op jit(solution)/shard_map/ppermute | solution.py:20
  247.0 7.1 %collective-permute-start.12 = (f32[1,4096]{1,0:T(1,128)S(1)}, f32[1,4096]{1,0:T(1,128)S(1)}, u32[]{:S(2)}, u32[]{:S(2)}) collective-permute-start(f32[1,4096]{1,0:T(1,128)S(1)} %get-tuple-element.30), channel_id=1, source_target_pairs={{4,0},{8,4},{12,8},{16,12},{20,16},{24,20},{28,24},{5,1},{9,5},{13... | collective-permute-start | bytes 49160 | tf_op jit(solution)/shard_map/ppermute | solution.py:23
  258.7 9.6 %copy-start.3 = (f32[128,4096]{1,0:T(8,128)}, f32[128,4096]{1,0:T(8,128)S(1)}, u32[]{:S(2)}) copy-start(f32[128,4096]{1,0:T(8,128)S(1)} %slice_add_fusion.2) | copy-start | bytes 6291460
  258.7 8.8 %collective-permute-start.13 = (f32[1,4096]{1,0:T(1,128)S(1)}, f32[1,4096]{1,0:T(1,128)S(1)}, u32[]{:S(2)}, u32[]{:S(2)}) collective-permute-start(f32[1,4096]{1,0:T(1,128)S(1)} %get-tuple-element.27), channel_id=1, source_target_pairs={{0,4},{4,8},{8,12},{12,16},{16,20},{20,24},{24,28},{1,5},{5,9},{9,... | collective-permute-start | bytes 49160 | tf_op jit(solution)/shard_map/ppermute | solution.py:20
  260.7 6.9 %collective-permute-start.14 = (f32[1,4096]{1,0:T(1,128)S(1)}, f32[1,4096]{1,0:T(1,128)S(1)}, u32[]{:S(2)}, u32[]{:S(2)}) collective-permute-start(f32[1,4096]{1,0:T(1,128)S(1)} %get-tuple-element.28), channel_id=1, source_target_pairs={{4,0},{8,4},{12,8},{16,12},{20,16},{24,20},{28,24},{5,1},{9,5},{13... | collective-permute-start | bytes 49160 | tf_op jit(solution)/shard_map/ppermute | solution.py:23
